TPU v7x, 256 devices: a whole 4x4x8 slice. The times are simulated.
256 devices in a mesh: ctx: 32 (over y_hi, z, core), grp: 2 (over y_lo), tp: 4 (over x).
Axes of the slice: x: 4, y: 4 (y_hi: 2, y_lo: 2; y = y_hi * 2 + y_lo), z: 8, core: 2. Of those that a mesh axis runs over, the one named last changes fastest.
Arguments:
- q_stretch: bfloat16 [2048, 8192], P('ctx', ('grp', 'tp')), may hold values from -200 to 200
- stretch_key_value: bfloat16 [2048, 2, 1024], P('ctx', None, ('grp', 'tp')), may hold values from -6 to 6
- context_key_value: bfloat16 [40960, 2, 1024], P('ctx', None, ('grp', 'tp')), may hold values from -6 to 6
- dec_q: bfloat16 [128, 2, 8192], P('ctx', None, ('grp', 'tp')), may hold values from -200 to 200
- dec_new: bfloat16 [128, 2, 2, 1024], P('ctx', None, None, ('grp', 'tp')), may hold values from -6 to 6
- pool_key_value: bfloat16 [1024, 128, 2, 1024], P('ctx', None, None, ('grp', 'tp')), may hold values from -6 to 6
- block_table: int32 [128, 8], replicated, may hold values from 0 to 1023, as said below
- cache_len: int32 [128], P('ctx'), may hold values from 1 to 1024, as said below
- w_out: bfloat16 [8192, 8192], P(('grp', 'tp'), 'ctx'), may hold values from -0.0625 to 0.0625
Outputs:
- pre_out: bfloat16 [2048, 8192], P('ctx', ('grp', 'tp'))
- dec_out: bfloat16 [128, 2, 8192], P(('grp', 'tp'), None, 'ctx')
Inputs may be any that keep to these rules, and one draw needn't show every extreme that they name: `block_table`: every pool block is named exactly once. The pool blocks of one index of ctx are an aligned run of 32; the decode rows of one index of ctx (an aligned run of 4 rows) name exactly 1 block of each such run. `cache_len`: some row has the full 1024 positions, and some other row has one.
All inputs are finite; a program needn't handle non-finite values.
Results may differ from a plain program's by a relative error of at most 0.035.
Values may be sent and summed in bfloat16 or wider, within the bound.
No kernel may reach another device: no remote copies, remote signals or barrier semaphores. Data moves between devices by JAX's collectives and lax.ppermute only.
A program may use at most 128 MiB of HBM per device.

v0:
```python
import math

import jax
import jax.numpy as jnp
from jax import lax
from jax.sharding import PartitionSpec as P

QUERY_HEADS = 64
VALUE_HEADS = 8
HEAD_SIZE = 128


def open_block(query_head_list, key_row_list, value_row_list, visible):
    scores = jnp.einsum(
        "qhgd,khd->qhgk", query_head_list, key_row_list, preferred_element_type=jnp.float32
    ) * (1.0 / math.sqrt(HEAD_SIZE))
    scores = jnp.where(visible[:, None, None, :], scores, -jnp.inf)
    top_score = jnp.max(scores, axis=-1)
    exponent = jnp.exp(scores - top_score[..., None])
    numerator = jnp.einsum(
        "qhgk,khd->qhgd",
        exponent.astype(jnp.bfloat16),
        value_row_list,
        preferred_element_type=jnp.float32,
    )
    return (top_score, jnp.sum(exponent, axis=-1), numerator)


def absorb(running, query_head_list, key_row_list, value_row_list):
    top_score, denominator, numerator = running
    scores = jnp.einsum(
        "qhgd,khd->qhgk", query_head_list, key_row_list, preferred_element_type=jnp.float32
    ) * (1.0 / math.sqrt(HEAD_SIZE))
    new_top = jnp.maximum(top_score, jnp.max(scores, axis=-1))
    factor = jnp.exp(top_score - new_top)
    exponent = jnp.exp(scores - new_top[..., None])
    numerator = numerator * factor[..., None] + jnp.einsum(
        "qhgk,khd->qhgd",
        exponent.astype(jnp.bfloat16),
        value_row_list,
        preferred_element_type=jnp.float32,
    )
    return (new_top, denominator * factor + jnp.sum(exponent, axis=-1), numerator)


def shards(
    q_stretch,
    stretch_key_value,
    context_key_value,
    dec_q,
    dec_new,
    pool_key_value,
    block_table,
    cache_len,
    w_out,
):
    device = lax.axis_index("ctx")
    cycle_size = lax.axis_size("ctx")
    kv_width = context_key_value.shape[2]
    kv_local = kv_width // HEAD_SIZE
    head_groups = QUERY_HEADS // VALUE_HEADS
    stretch_dev = q_stretch.shape[0]
    stretch_all = lax.all_gather(stretch_key_value, "ctx", axis=0, tiled=True)
    stretch_total = stretch_all.shape[0]
    stretch_keys = stretch_all[:, 0].reshape(stretch_total, kv_local, HEAD_SIZE)
    stretch_values = stretch_all[:, 1].reshape(stretch_total, kv_local, HEAD_SIZE)
    own_heads = q_stretch.reshape(stretch_dev, kv_local, head_groups, HEAD_SIZE)
    own_rows = device * stretch_dev + jnp.arange(stretch_dev, dtype=jnp.int32)
    visible = jnp.arange(stretch_total, dtype=jnp.int32)[None, :] <= own_rows[:, None]
    stretch_stats = open_block(own_heads, stretch_keys, stretch_values, visible)
    shard_rows = lax.all_gather(context_key_value, "ctx", axis=0, tiled=True)
    count_rows = shard_rows.shape[0]
    key_row_list = shard_rows[:, 0].reshape(count_rows, kv_local, HEAD_SIZE)
    value_row_list = shard_rows[:, 1].reshape(count_rows, kv_local, HEAD_SIZE)
    key_blocks = key_row_list.reshape(count_rows // 4096, 4096, kv_local, HEAD_SIZE)
    value_blocks = value_row_list.reshape(count_rows // 4096, 4096, kv_local, HEAD_SIZE)

    def through(carried, block_pair):
        return (absorb(carried, own_heads, block_pair[0], block_pair[1]), None)

    finished, unused = lax.scan(through, stretch_stats, (key_blocks, value_blocks))
    top_score, denominator, numerator = finished
    pre_out = (
        (numerator / denominator[..., None])
        .astype(jnp.bfloat16)
        .reshape(stretch_dev, kv_local * head_groups * HEAD_SIZE)
    )
    rows_dev = dec_q.shape[0]
    nblk = block_table.shape[1]
    entries = rows_dev * nblk
    pool_dev = pool_key_value.shape[0]
    block_size = pool_key_value.shape[1]
    cap_count = entries // cycle_size
    table_all = block_table.reshape(cycle_size, entries)
    source_all = table_all // pool_dev
    arrival_all = jnp.argsort(source_all, axis=1, stable=True)
    ranked = jnp.take_along_axis(table_all, arrival_all, axis=1).reshape(
        cycle_size, cycle_size, cap_count
    )
    wanted = lax.dynamic_index_in_dim(ranked, device, 1, keepdims=False) - device * pool_dev
    arrival = lax.dynamic_index_in_dim(arrival_all, device, 0, keepdims=False)
    restore = jnp.argsort(arrival)
    query_head_list = dec_q.reshape(rows_dev, 2, kv_local, head_groups, HEAD_SIZE)
    scale = 1.0 / math.sqrt(HEAD_SIZE)
    outgoing = jnp.take(pool_key_value, wanted.reshape(cycle_size * cap_count), axis=0)
    incoming = lax.all_to_all(outgoing, "ctx", split_axis=0, concat_axis=0, tiled=True)
    placed = jnp.take(incoming, restore, axis=0)
    cache_span = nblk * block_size
    cache_row_list = placed.reshape(rows_dev, cache_span, 2, kv_width)
    key_row_list = jnp.concatenate([cache_row_list[:, :, 0], dec_new[:, :, 0]], axis=1).reshape(
        rows_dev, cache_span + 2, kv_local, HEAD_SIZE
    )
    value_row_list = jnp.concatenate([cache_row_list[:, :, 1], dec_new[:, :, 1]], axis=1).reshape(
        rows_dev, cache_span + 2, kv_local, HEAD_SIZE
    )
    scores = (
        jnp.einsum(
            "rthgd,rkhd->rthgk", query_head_list, key_row_list, preferred_element_type=jnp.float32
        )
        * scale
    )
    positions = jnp.arange(cache_span + 2, dtype=jnp.int32)
    step_index = jnp.arange(2, dtype=jnp.int32)
    allowed = jnp.where(
        positions[None, None, :] < cache_span,
        positions[None, None, :] < cache_len[:, None, None],
        positions[None, None, :] - cache_span <= step_index[None, :, None],
    )
    scores = jnp.where(allowed[:, :, None, None, :], scores, -jnp.inf)
    top_score = jnp.max(scores, axis=-1, keepdims=True)
    exponent = jnp.exp(scores - top_score)
    dec_sum = jnp.sum(exponent, axis=-1, keepdims=True)
    summed = jnp.einsum(
        "rthgk,rkhd->rthgd",
        exponent.astype(jnp.bfloat16),
        value_row_list,
        preferred_element_type=jnp.float32,
    )
    dec_attn = (
        (summed / dec_sum)
        .astype(jnp.bfloat16)
        .reshape(rows_dev, 2, kv_local * head_groups * HEAD_SIZE)
    )
    partial_out = jnp.einsum(
        "rtc,cd->rtd",
        lax.all_gather(dec_attn, "ctx", axis=0, tiled=True),
        w_out,
        preferred_element_type=jnp.float32,
    )
    dec_out = lax.psum_scatter(
        partial_out.astype(jnp.bfloat16), ("grp", "tp"), scatter_dimension=0, tiled=True
    )
    return (pre_out, dec_out)


def solution(mesh):
    placed = (
        P("ctx", ("grp", "tp")),
        P("ctx", None, ("grp", "tp")),
        P("ctx", None, ("grp", "tp")),
        P("ctx", None, ("grp", "tp")),
        P("ctx", None, None, ("grp", "tp")),
        P("ctx", None, None, ("grp", "tp")),
        P(),
        P("ctx"),
        P(("grp", "tp"), "ctx"),
    )
    return jax.shard_map(
        shards,
        mesh=mesh,
        in_specs=placed,
        out_specs=(P("ctx", ("grp", "tp")), P(("grp", "tp"), None, "ctx")),
        check_vma=False,
    )
```

profile of v0, /device:TPU:1, one launch (start us, length us, event | category | flops | bytes accessed | tf_op | source)
XLA Modules:
  0.0 398.4 jit_solution(8827869259471583168)
XLA Ops:
  10.1 7.1 %gather_fusion = s32[1024]{0:T(1024)S(1)} fusion(s32[32,32]{1,0:T(8,128)S(1)} %reshape.208, s32[1024]{0:T(1024)S(1)} %reshape.231), kind=kCustom, calls=%fused_computation.2 | custom fusion | bytes 16384 | tf_op jit(solution)/shard_map/jit(take_along_axis)/gather | solution.py:97
  17.5 6.2 %gather_fusion.1 = bf16[32,128,2,128]{3,2,1,0:T(2,128)(2,1)} fusion(bf16[32,128,2,128]{3,2,1,0:T(2,128)(2,1)S(1)} %copy-done, s32[1024]{0:T(1024)S(1)} %pad_clamp_fusion.1), kind=kCustom, calls=%fused_computation.clone | custom fusion | bytes 4194432 | tf_op jit(solution)/shard_map/jit(_take)/gather | solution.py:105
  23.7 4.9 %broadcast_select_fusion.1 = bf16[32,128,2,128]{3,2,1,0:T(2,128)(2,1)} fusion(bf16[32,128,2,128]{3,2,1,0:T(2,128)(2,1)} %gather_fusion.1, pred[32]{0:T(512)(128)(4,1)S(1)} %get-tuple-element.99), kind=kLoop, calls=%fused_computation.28 | loop fusion | flops 1048576 | bytes 4194336 | tf_op jit(solution)/shard_map/jit(_take)/select_n | solution.py:105
  28.6 12.8 %all-to-all-start = ((bf16[32,128,2,128]{3,2,1,0:T(2,128)(2,1)}), bf16[32,128,2,128]{3,2,1,0:T(2,128)(2,1)S(1)}, u32[]{:S(2)}, u32[]{:S(2)}) async-start(bf16[32,128,2,128]{3,2,1,0:T(2,128)(2,1)} %broadcast_select_fusion.1), calls=%async_computation | async-start | bytes 4194304 | tf_op jit(solution)/shard_map/all_to_all | solution.py:106
  44.2 49.3 %all-to-all-done = bf16[32,128,2,128]{3,2,1,0:T(2,128)(2,1)S(1)} async-done(((bf16[32,128,2,128]{3,2,1,0:T(2,128)(2,1)}), bf16[32,128,2,128]{3,2,1,0:T(2,128)(2,1)S(1)}, u32[]{:S(2)}, u32[]{:S(2)}) %all-to-all-start) | async-done | bytes 2097184 | tf_op jit(solution)/shard_map/all_to_all | solution.py:106
  93.5 6.2 %gather_fusion.2 = bf16[32,128,2,128]{3,2,1,0:T(2,128)(2,1)} fusion(bf16[32,128,2,128]{3,2,1,0:T(2,128)(2,1)S(1)} %all-to-all-done, s32[1024]{0:T(1024)S(1)} %pad_clamp_fusion), kind=kCustom, calls=%fused_computation.1.clone | custom fusion | bytes 4194432 | tf_op jit(solution)/shard_map/jit(_take)/gather | solution.py:107
  99.7 3.5 broadcast_select_fusion
  104.9 42.0 %all_gather.11 = bf16[128,2,1024]{2,1,0:T(2,128)(2,1)S(1)} all-gather(bf16[4,2,1024]{2,1,0:T(2,128)(2,1)S(1)} %reshape.214), channel_id=1, replica_groups=mesh['ctx'=32,'grp'=2,'tp'=4] {'ctx'}, dimensions={0}, use_global_device_ids=true | all-gather | bytes 540672 | tf_op jit(solution)/shard_map/all_gather | solution.py:146
  153.1 22.7 %reduce-scatter.2.cloned.1.call-done = bf16[16,2,256]{2,0,1:T(8,128)(2,1)} async-done(((bf16[128,2,256]{2,0,1:T(8,128)(2,1)}), bf16[16,2,256]{2,0,1:T(8,128)(2,1)}) %reduce-scatter.2.cloned.1.call-update) | async-done | bytes 16400 | tf_op jit(solution)/shard_map/reduce_scatter | solution.py:150
  177.2 127.2 %all-gather.5.cloned.1.call-done = bf16[40960,2,128]{2,0,1:T(8,128)(2,1)} async-done(((bf16[1280,2,128]{2,0,1:T(8,128)(2,1)}), bf16[40960,2,128]{2,0,1:T(8,128)(2,1)}) %all-gather.5.cloned.1.call-update) | async-done | bytes 20971536 | tf_op jit(solution)/shard_map/all_gather | solution.py:71
  304.3 15.7 %fusion.53 = (bf16[40960,1,128]{2,0,1:T(8,128)(2,1)}, bf16[40960,1,128]{2,0,1:T(8,128)(2,1)}) fusion(bf16[40960,2,128]{2,0,1:T(8,128)(2,1)} %all-gather.5.cloned.1.call-done), kind=kLoop, calls=%fused_computation.94 | loop fusion | bytes 41943040 | tf_op jit(solution)/shard_map/slice | solution.py:74
  320.0 69.3 %while.14 = (s32[]{:T(128)}, f32[64,1,8]{0,2,1:T(8,128)S(1)}, f32[64,1,8]{0,2,1:T(8,128)S(1)}, f32[64,1,8,128]{3,0,2,1:T(8,128)S(1)}, bf16[10,4096,1,128]{3,1,2,...) while((s32[]{:T(128)}, f32[64,1,8]{0,2,1:T(8,128)S(1)}, ...), condition=%wide.region_5.6_spmd, body=%wide.region_2.5_spmd.sunk | while | flops 1090651648 | bytes 27951204 | solution.py:81
  320.0 2.5 bitcast_reduce_fusion.2
  324.1 2.8 fusion.68
  326.9 2.6 bitcast_reduce_fusion.2
  331.0 2.8 fusion.68
  333.9 2.6 bitcast_reduce_fusion.2
  337.9 2.8 fusion.68
  340.8 2.6 bitcast_reduce_fusion.2
  344.9 2.8 fusion.68
  347.7 2.6 bitcast_reduce_fusion.2
  351.8 2.8 fusion.68
  354.7 2.6 bitcast_reduce_fusion.2
  358.8 2.8 fusion.68
  361.6 2.6 bitcast_reduce_fusion.2
  365.7 2.8 fusion.68
  368.5 2.6 bitcast_reduce_fusion.2
  372.6 2.8 fusion.68
  375.5 2.6 bitcast_reduce_fusion.2
  379.6 2.8 fusion.68
  382.4 2.6 bitcast_reduce_fusion.2
  386.5 2.8 fusion.68
  (116 shorter events, 31.0 us)
Async XLA Ops:
  8.0 9.5 %copy-start = (bf16[32,128,2,128]{3,2,1,0:T(2,128)(2,1)S(1)}, bf16[32,128,2,128]{3,2,1,0:T(2,128)(2,1)}, u32[]{:S(2)}) copy-start(bf16[32,128,2,128]{3,2,1,0:T(2,128)(2,1)} %param.18) | copy-start | bytes 6291460
  23.7 17.7 %copy-start.5 = (bf16[64,2,128]{2,1,0:T(2,128)(2,1)S(1)}, bf16[64,2,128]{2,1,0:T(2,128)(2,1)}, u32[]{:S(2)}) copy-start(bf16[64,2,128]{2,1,0:T(2,128)(2,1)} %param.14) | copy-start | bytes 98308
  23.7 18.5 %copy-start.6 = (bf16[4,2,1024]{2,1,0:T(2,128)(2,1)S(1)}, bf16[4,2,1024]{2,1,0:T(2,128)(2,1)}, u32[]{:S(2)}) copy-start(bf16[4,2,1024]{2,1,0:T(2,128)(2,1)} %param.16) | copy-start | bytes 49156
  23.7 20.3 %copy-start.7 = (bf16[4,2,2,128]{3,2,1,0:T(2,128)(2,1)S(1)}, bf16[4,2,2,128]{3,2,1,0:T(2,128)(2,1)}, u32[]{:S(2)}) copy-start(bf16[4,2,2,128]{3,2,1,0:T(2,128)(2,1)} %param.17) | copy-start | bytes 12292
  23.7 20.4 %copy-start.8 = (s32[4]{0:T(128)S(1)}, s32[4]{0:T(128)}, u32[]{:S(2)}) copy-start(s32[4]{0:T(128)} %param.20) | copy-start | bytes 52
  28.6 64.9 %all-to-all-start = ((bf16[32,128,2,128]{3,2,1,0:T(2,128)(2,1)}), bf16[32,128,2,128]{3,2,1,0:T(2,128)(2,1)S(1)}, u32[]{:S(2)}, u32[]{:S(2)}) async-start(bf16[32,128,2,128]{3,2,1,0:T(2,128)(2,1)} %broadcast_select_fusion.1), calls=%async_computation | async-start | bytes 4194304 | tf_op jit(solution)/shard_map/all_to_all | solution.py:106
  41.4 107.8 %all-gather.3.cloned.1.call-start = ((), (), s32[]{:S(2)}) async-start(), calls=%async_computation.2 | async-start | bytes 1081344 | tf_op jit(solution)/shard_map/all_gather | solution.py:63
  42.1 133.7 %reduce-scatter.2.cloned.1.call-start = ((), (), s32[]{:S(2)}) async-start(), calls=%async_computation.4 | async-start | bytes 147456 | tf_op jit(solution)/shard_map/reduce_scatter | solution.py:150
  103.7 43.2 %copy-start.9 = (bf16[1024,256]{1,0:T(8,128)(2,1)S(1)}, bf16[1024,256]{1,0:T(8,128)(2,1)}, u32[]{:S(2)}) copy-start(bf16[1024,256]{1,0:T(8,128)(2,1)} %param.21) | copy-start | bytes 1572868
  103.9 44.1 %copy-start.2 = (bf16[1280,2,128]{2,1,0:T(2,128)(2,1)S(1)}, bf16[1280,2,128]{2,1,0:T(2,128)(2,1)}, u32[]{:S(2)}) copy-start(bf16[1280,2,128]{2,1,0:T(2,128)(2,1)} %param.15) | copy-start | bytes 1966084
  103.9 45.0 %copy-start.4 = (bf16[64,1024]{1,0:T(8,128)(2,1)S(1)}, bf16[64,1024]{1,0:T(8,128)(2,1)}, u32[]{:S(2)}) copy-start(bf16[64,1024]{1,0:T(8,128)(2,1)} %param.13) | copy-start | bytes 393220
  147.9 156.4 %all-gather.5.cloned.1.call-start = ((), (), s32[]{:S(2)}) async-start(), calls=%async_computation.3 | async-start | bytes 21626880 | tf_op jit(solution)/shard_map/all_gather | solution.py:71
  151.1 1.2 copy-start.3
  389.3 1.6 copy-start.1
Sparse Core Ops, SparseCore 0:
  45.0 83.6 all-gather.2
  151.6 152.7 all-gather.4
Sparse Core Ops, SparseCore 1:
  148.0 27.8 reduce-scatter.1
where the time goes:
time: 400 us; the launch traced here: 398 us
  waiting for transfers between devices  199 us (50%)
  matrix products  58.3 us (15%)
  local copies, waits for them, and re-layouts  42.5 us (11%)
  blocking collectives  42 us (10%)
  other arithmetic  27.4 us (7%)
  between operations  15.8 us (4%)
  starting transfers between devices  12.9 us (3%)
    all_gather x1, waiting for transfers between devices, shards(): shard_rows = lax.all_gather(context_key_value, 'ctx', axis=0, tiled=True)  127 us
    all_to_all x1, waiting for transfers between devices, shards(): lax.all_to_all(outgoing, 'ctx', split_axis=0, concat_axis=0, tiled=True)  49.3 us
    all_gather x1, blocking collectives, shards(): lax.all_gather(dec_attn, 'ctx', axis=0, tiled=True)  42 us
    dot_general x10, matrix products, absorb(): jnp.einsum('qhgk,khd->qhgd', exponent.astype(jnp.bfloat16), value_row_lis...  28.3 us
    dot_general x10, matrix products, absorb(): jnp.einsum('qhgd,khd->qhgk', query_head_list, key_row_list, preferred_ele...  25.5 us
    reduce_scatter x1, waiting for transfers between devices, shards(): lax.psum_scatter(partial_out.astype(jnp.bfloat16), ('grp', 'tp'), scatter...  22.7 us
    slice x1, local copies, waits for them, and re-layouts, shards(): value_row_list = shard_rows[:, 1].reshape(count_rows, kv_local, HEAD_SIZE)  15.7 us
    reduce_sum x10, other arithmetic, absorb(): jnp.sum(exponent, axis=-1)  15 us
  transfers between devices with their start and end apart: 4, of which 3 were waited for; matrix products, arithmetic and copies ran while one was open for 5% of the time, Pallas kernels for 0%

commit v1 on v0

v1 whole, which is shorter than its diff:
```python
import functools
import math

import jax
import jax.numpy as jnp
from jax import lax
from jax.experimental import pallas as pl
from jax.experimental.pallas import tpu as pltpu
from jax.sharding import PartitionSpec as P

HEAD_SIZE = 128
CORES = 2
Z_CHIPS = 8
CTX = ("y", "z", "core")
SCALE = math.log2(math.e) / math.sqrt(HEAD_SIZE)
LOWEST = -1e30
F32 = jnp.float32
BF16 = jnp.bfloat16
TILE = 256
VMEM = pl.BlockSpec(memory_space=pltpu.VMEM)
SMEM = pl.BlockSpec(memory_space=pltpu.SMEM)


def params(mib):
    return pltpu.CompilerParams(vmem_limit_bytes=mib * 1024 * 1024)


def dot_nt(a, b):
    return lax.dot_general(a, b, (((1,), (1,)), ((), ())), preferred_element_type=F32)


def dot_nn(a, b):
    return lax.dot_general(a, b, (((1,), (0,)), ((), ())), preferred_element_type=F32)


def split_body(context_ref, stretch_ref, out_ref):
    def split(rows, at):
        count = rows.shape[0]
        half = count // 2
        i = lax.broadcasted_iota(jnp.int32, (count, count), 0)
        j = lax.broadcasted_iota(jnp.int32, (count, count), 1)
        source = jnp.where(i < half, 2 * i, 2 * (i - half) + 1)
        pick = jnp.where(j == source, 1.0, 0.0).astype(BF16)
        parted = dot_nn(pick, rows).astype(BF16)
        out_ref[0, at : at + half, :] = parted[:half]
        out_ref[1, at : at + half, :] = parted[half:]

    total = context_ref.shape[0]
    for start in range(0, total, 256):
        split(context_ref[start : start + 256, :], start // 2)
    split(stretch_ref[...], total // 2)


def split_keys_values(context, stretch):
    rows = (context.shape[0] + stretch.shape[0]) // 2
    return pl.pallas_call(
        split_body,
        out_shape=jax.ShapeDtypeStruct((2, rows, HEAD_SIZE), BF16),
        in_specs=[VMEM, VMEM],
        out_specs=VMEM,
        compiler_params=params(16),
        name="split_keys_values",
    )(context, stretch)


def attend_body(first_head, deltas_ref, q_ref, kv_ref, out_ref, s_ref, p_ref, v_ref, top_ref):
    tiles, stretch = q_ref.shape[:2]
    sets = kv_ref.shape[0]
    keys = kv_ref.shape[2] - stretch
    heads_tile = TILE // stretch
    chunk_size = 256

    v_ref[:, HEAD_SIZE:] = jnp.ones((v_ref.shape[0], HEAD_SIZE), BF16)
    for n in range(sets):
        v_ref[n * keys : (n + 1) * keys, :HEAD_SIZE] = kv_ref[n, 1, :keys, :]
        v_ref[sets * keys + n * stretch : sets * keys + (n + 1) * stretch, :HEAD_SIZE] = kv_ref[n, 1, keys:, :]

    chunks = []
    for n in range(sets):
        for start in range(0, keys, chunk_size):
            chunks.append((n, start, n * keys + start, chunk_size))
    chunks.append((None, 0, sets * keys, sets * stretch))

    def queries(t):
        heads = range(first_head, first_head + heads_tile)
        return jnp.concatenate([q_ref[t, :, h * HEAD_SIZE : (h + 1) * HEAD_SIZE] for h in heads], axis=0)

    def score(t, slot, q, top, chunk):
        n, start, at, size = chunk
        if n is None:
            k = jnp.concatenate([kv_ref[m, 0, keys:, :] for m in range(sets)], axis=0)
        else:
            k = kv_ref[n, 0, start : start + size, :]
        s = dot_nt(q, k)
        if n is None:
            row = lax.rem(lax.broadcasted_iota(jnp.int32, (TILE, size), 0), stretch)
            col = lax.broadcasted_iota(jnp.int32, (TILE, size), 1)
            bound = deltas_ref[t * sets + sets - 1] + (sets - 1) * stretch - col
            for m in reversed(range(sets - 1)):
                bound = jnp.where(col < (m + 1) * stretch, deltas_ref[t * sets + m] + m * stretch - col, bound)
            s = jnp.where(row + bound >= 0, s, LOWEST)
        s_ref[slot, :, at : at + size] = s
        for c in range(0, size, HEAD_SIZE):
            part = s[:, c : c + HEAD_SIZE]
            top = part if top is None else jnp.maximum(top, part)
        return top

    def settle(slot, top):
        top_ref[slot] = jnp.broadcast_to(jnp.max(top, axis=1, keepdims=True), (TILE, HEAD_SIZE)) * SCALE

    def weigh(slot, top, chunk):
        at, size = chunk[2], chunk[3]
        for c in range(at, at + size, HEAD_SIZE):
            p_ref[slot, :, c : c + HEAD_SIZE] = jnp.exp2(s_ref[slot, :, c : c + HEAD_SIZE] * SCALE - top).astype(BF16)

    def finish(t, slot, top):
        total = dot_nn(p_ref[slot], v_ref[...])
        weight = total[:, HEAD_SIZE:]
        out_ref[t, :TILE, :] = (total[:, :HEAD_SIZE] / weight).astype(BF16)
        level = top + jnp.log2(weight)
        i = lax.broadcasted_iota(jnp.int32, (HEAD_SIZE, HEAD_SIZE), 0)
        j = lax.broadcasted_iota(jnp.int32, (HEAD_SIZE, HEAD_SIZE), 1)
        rows = []
        for g in range(TILE // HEAD_SIZE):
            part = jnp.where(i == j, level[g * HEAD_SIZE : (g + 1) * HEAD_SIZE], 0.0)
            rows.append(jnp.sum(part, axis=0, keepdims=True))
        k = lax.broadcasted_iota(jnp.int32, (8, HEAD_SIZE), 0)
        level = jnp.where(k == 0, rows[0], jnp.where(k == 1, rows[1], 0.0))
        high = level.astype(BF16).astype(F32)
        rest = level - high
        middle = rest.astype(BF16).astype(F32)
        pieces = [high, middle, rest - middle, jnp.zeros_like(level)]
        out_ref[t, TILE:, :] = jnp.concatenate(pieces, axis=0).astype(BF16)

    def step(t, slot, following):
        top = top_ref[slot]
        coming = None
        if following is not None:
            q = queries(following)
        for chunk in chunks:
            weigh(slot, top, chunk)
            if following is not None:
                coming = score(following, 1 - slot, q, coming, chunk)
        if following is not None:
            settle(1 - slot, coming)
        finish(t, slot, top)

    top = None
    q = queries(0)
    for chunk in chunks:
        top = score(0, 0, q, top, chunk)
    settle(0, top)

    def pair(i, carry):
        step(2 * i, 0, 2 * i + 1)
        step(2 * i + 1, 1, 2 * i + 2)
        return carry

    lax.fori_loop(0, tiles // 2 - 1, pair, 0)
    step(tiles - 2, 0, tiles - 1)
    step(tiles - 1, 1, None)


def attend(first_head, deltas, queries, kv):
    tiles, stretch, _ = queries.shape
    keys = kv.shape[0] * kv.shape[2]
    return pl.pallas_call(
        functools.partial(attend_body, first_head),
        out_shape=jax.ShapeDtypeStruct((tiles, TILE + 32, HEAD_SIZE), BF16),
        in_specs=[SMEM, VMEM, VMEM],
        out_specs=VMEM,
        scratch_shapes=[
            pltpu.VMEM((2, TILE, keys), F32),
            pltpu.VMEM((2, TILE, keys), BF16),
            pltpu.VMEM((keys, 2 * HEAD_SIZE), BF16),
            pltpu.VMEM((2, TILE, HEAD_SIZE), F32),
        ],
        compiler_params=params(40),
        cost_estimate=pl.CostEstimate(
            flops=8 * tiles * TILE * keys * HEAD_SIZE,
            bytes_accessed=4 * keys * HEAD_SIZE,
            transcendentals=tiles * TILE * keys,
        ),
        name="attend",
    )(deltas, queries, kv)


def merge_body(*refs):
    out_ref = refs[-1]
    stretch = out_ref.shape[0]
    i = lax.broadcasted_iota(jnp.int32, (HEAD_SIZE, HEAD_SIZE), 0)
    j = lax.broadcasted_iota(jnp.int32, (HEAD_SIZE, HEAD_SIZE), 1)
    head = 0
    for ref in refs[:-1]:
        count = ref.shape[0]
        levels = []
        for n in range(count):
            stat = ref[n, TILE:, :].astype(F32)
            levels.append(stat[0:8] + stat[8:16] + stat[16:24])
        top = functools.reduce(jnp.maximum, levels)
        weights = [jnp.exp2(level - top) for level in levels]
        total = functools.reduce(jnp.add, weights)
        weights = [weight / total for weight in weights]
        for g in range(TILE // HEAD_SIZE):
            mixed = None
            for n in range(count):
                column = jnp.sum(jnp.where(i == j, weights[n][g : g + 1, :], 0.0), axis=1, keepdims=True)
                term = column * ref[n, g * HEAD_SIZE : (g + 1) * HEAD_SIZE, :].astype(F32)
                mixed = term if mixed is None else mixed + term
            mixed = mixed.astype(BF16)
            for h in range(HEAD_SIZE // stretch):
                out_ref[:, head * HEAD_SIZE : (head + 1) * HEAD_SIZE] = mixed[h * stretch : (h + 1) * stretch]
                head += 1


def merge(parts, stretch):
    width = len(parts) * TILE // stretch * HEAD_SIZE
    return pl.pallas_call(
        merge_body,
        out_shape=jax.ShapeDtypeStruct((stretch, width), BF16),
        in_specs=[VMEM] * len(parts),
        out_specs=VMEM,
        compiler_params=params(16),
        name="merge_parts",
    )(*parts)


def look_body(place_ref, ask_ref, pool_ref, out_ref, s_ref, p_ref):
    owners = ask_ref.shape[0]
    half = ask_ref.shape[1] // 2
    span = pool_ref.shape[1]
    for d in range(owners):
        s_ref[d * half : (d + 1) * half, :] = dot_nt(ask_ref[d, :half, :], pool_ref[place_ref[d]])
    col = lax.broadcasted_iota(jnp.int32, (half, span), 1)
    lane = lax.broadcasted_iota(jnp.int32, (half, HEAD_SIZE), 1)
    even = (col & 1) == 0
    for d in range(owners):
        limit = ask_ref[d, half:, :].astype(F32) * 2.0
        limit = jnp.concatenate([limit] * (span // HEAD_SIZE), axis=1)
        allowed = even & (col.astype(F32) < limit)
        s = jnp.where(allowed, s_ref[d * half : (d + 1) * half, :], LOWEST)
        top = jnp.max(s, axis=1, keepdims=True)
        p = jnp.where(allowed, jnp.exp2((s - top) * SCALE), 0.0)
        total = jnp.sum(p, axis=1, keepdims=True)
        p_ref[d * half : (d + 1) * half, :] = pltpu.roll(p, 1, 1).astype(BF16)
        seen = total > 0.0
        level = jnp.where(seen, top * SCALE + jnp.log2(jnp.where(seen, total, 1.0)), LOWEST)
        level = jnp.broadcast_to(level, (half, HEAD_SIZE))
        high = level.astype(BF16).astype(F32)
        rest = level - high
        middle = rest.astype(BF16).astype(F32)
        low = rest - middle
        stat = jnp.where(lane == 0, high, jnp.where(lane == 1, middle, jnp.where(lane == 2, low, 0.0)))
        out_ref[d, half:, :] = stat.astype(BF16)
        s_ref[d * half : (d + 1) * half, :HEAD_SIZE] = jnp.broadcast_to(
            jnp.where(seen, 1.0 / jnp.where(seen, total, 1.0), 0.0), (half, HEAD_SIZE)
        )
    for d in range(owners):
        o = dot_nn(p_ref[d * half : (d + 1) * half, :], pool_ref[place_ref[d]])
        out_ref[d, :half, :] = (o * s_ref[d * half : (d + 1) * half, :HEAD_SIZE]).astype(BF16)


def look(place, ask, pool):
    owners, rows, width = ask.shape
    span = pool.shape[1]
    return pl.pallas_call(
        look_body,
        out_shape=jax.ShapeDtypeStruct(ask.shape, BF16),
        in_specs=[SMEM, VMEM, VMEM],
        out_specs=VMEM,
        scratch_shapes=[
            pltpu.VMEM((owners * rows // 2, span), F32),
            pltpu.VMEM((owners * rows // 2, span), BF16),
        ],
        compiler_params=params(24),
        cost_estimate=pl.CostEstimate(
            flops=16 * owners * rows * span * width, bytes_accessed=2 * owners * span * width, transcendentals=0
        ),
        name="look_in_blocks",
    )(place, ask, pool)


def gather_body(row_ref, answer_ref, q_ref, new_ref, out_ref, level_ref, top_ref, sum_ref, acc_ref, flat_ref):
    holders = answer_ref.shape[0]
    rows, lists = q_ref.shape[0], q_ref.shape[1]
    heads = lists // 2
    lane = lax.broadcasted_iota(jnp.int32, (lists, HEAD_SIZE), 1)
    later = lax.broadcasted_iota(jnp.int32, (lists, HEAD_SIZE), 0) >= heads
    own = []
    for r in range(rows):
        q = q_ref[r].astype(F32)
        new = new_ref[r].astype(F32)
        scores = []
        for t in range(2):
            s = jnp.sum(q * new[2 * t : 2 * t + 1, :], axis=1, keepdims=True) * SCALE
            scores.append(jnp.broadcast_to(s, (lists, HEAD_SIZE)))
        scores[1] = jnp.where(later, scores[1], LOWEST)
        top_ref[r] = jnp.maximum(scores[0], scores[1])
        own.append((scores, new))
    for d in range(holders):
        stat = answer_ref[d, lists:, :].astype(F32)
        level = jnp.sum(jnp.where(lane < 3, stat, 0.0), axis=1, keepdims=True)
        level_ref[d] = jnp.broadcast_to(level, (lists, HEAD_SIZE))
    for d in range(holders):
        r = row_ref[d]
        top_ref[r] = jnp.maximum(top_ref[r], level_ref[d])
    for r in range(rows):
        scores, new = own[r]
        first = jnp.exp2(scores[0] - top_ref[r])
        second = jnp.exp2(scores[1] - top_ref[r])
        sum_ref[r] = first + second
        acc_ref[r] = first * new[1:2, :] + second * new[3:4, :]
    for d in range(holders):
        r = row_ref[d]
        weight = jnp.exp2(level_ref[d] - top_ref[r])
        sum_ref[r] = sum_ref[r] + weight
        acc_ref[r] = acc_ref[r] + weight * answer_ref[d, :lists, :].astype(F32)
    for r in range(rows):
        o = acc_ref[r] / sum_ref[r]
        for t in range(2):
            for h in range(heads):
                flat_ref[2 * r + t : 2 * r + t + 1, h * HEAD_SIZE : (h + 1) * HEAD_SIZE] = o[
                    t * heads + h : t * heads + h + 1, :
                ]
    out_ref[...] = flat_ref[...].astype(BF16)


def gather_answers(row_of, answer, q, new):
    rows, lists, width = q.shape
    holders = answer.shape[0]
    heads = lists // 2
    state = pltpu.VMEM((rows, lists, width), F32)
    return pl.pallas_call(
        gather_body,
        out_shape=jax.ShapeDtypeStruct((2 * rows, heads * width), BF16),
        in_specs=[SMEM, VMEM, VMEM, VMEM],
        out_specs=VMEM,
        scratch_shapes=[
            pltpu.VMEM((holders, lists, width), F32),
            state,
            state,
            state,
            pltpu.VMEM((2 * rows, heads * width), F32),
        ],
        compiler_params=params(16),
        name="gather_answers",
    )(row_of, answer, q, new)


def shards(
    q_stretch,
    stretch_key_value,
    context_key_value,
    dec_q,
    dec_new,
    pool_key_value,
    block_table,
    cache_len,
    w_out,
):
    me = lax.axis_index(CTX)
    cycle = lax.axis_size(CTX)
    stretch = q_stretch.shape[0]

    q_all = lax.all_gather(q_stretch, "z", axis=0)
    kv = split_keys_values(
        context_key_value.reshape(-1, HEAD_SIZE), stretch_key_value.reshape(-1, HEAD_SIZE)
    )
    kv_all = lax.all_gather(kv, ("y", "core"), axis=0)

    rows_dev, nblk = dec_q.shape[0], block_table.shape[1]
    entries = rows_dev * nblk
    pool_dev, block_size = pool_key_value.shape[:2]
    heads = dec_q.shape[2] // HEAD_SIZE
    table = block_table.reshape(cycle, entries)
    source, slot = table // pool_dev, table % pool_dev
    place = jnp.sum(jnp.where(source == me, slot, 0), axis=1)
    mine = lax.dynamic_index_in_dim(source, me, 0, keepdims=False)
    entry_ids = jnp.arange(entries, dtype=jnp.int32)
    holder_ids = jnp.arange(cycle, dtype=jnp.int32)
    entry_of = jnp.sum(jnp.where(mine[None, :] == holder_ids[:, None], entry_ids[None, :], 0), axis=1)
    row_of = entry_of // nblk
    block_of = entry_of % nblk
    own_rows = jnp.arange(rows_dev, dtype=jnp.int32)
    length_of = jnp.sum(jnp.where(row_of[:, None] == own_rows[None, :], cache_len[None, :], 0), axis=1)
    count_of = jnp.clip(length_of - block_of * block_size, 0, block_size).astype(BF16)
    lists = 2 * heads
    q_rows = dec_q.reshape(rows_dev, lists, HEAD_SIZE)
    asked = q_rows[0][None]
    for r in range(1, rows_dev):
        asked = jnp.where((row_of == r)[:, None, None], q_rows[r][None], asked)
    asked = jnp.broadcast_to(asked, (cycle, lists, HEAD_SIZE))
    counts = jnp.broadcast_to(count_of[:, None, None], (cycle, lists, HEAD_SIZE))
    ask = jnp.concatenate([asked, counts], axis=1)
    ask = lax.all_to_all(ask, CTX, split_axis=0, concat_axis=0, tiled=True)

    look_out = look(place, ask, pool_key_value.reshape(pool_dev, 2 * block_size, HEAD_SIZE))
    answer = lax.all_to_all(look_out, CTX, split_axis=0, concat_axis=0, tiled=True)
    attn = gather_answers(row_of, answer, q_rows, dec_new.reshape(rows_dev, 4, HEAD_SIZE))
    everyone = lax.all_gather(attn, CTX, axis=0, tiled=True)

    y, z, core = (lax.axis_index(name) for name in CTX)
    asker = (y * Z_CHIPS + jnp.arange(Z_CHIPS, dtype=jnp.int32)) * CORES + core
    shard = jnp.arange(2 * CORES, dtype=jnp.int32)
    shard = ((shard // CORES) * Z_CHIPS + z) * CORES + shard % CORES
    deltas = ((asker[:, None] - shard[None, :]) * stretch).reshape(-1)
    parts = []
    heads_tile = TILE // stretch
    deltas, _ = lax.optimization_barrier((deltas, attn))
    for first_head in range(0, heads, heads_tile):
        part = attend(first_head, deltas, q_all, kv_all)
        deltas, part = lax.optimization_barrier((deltas, part))
        parts.append(lax.all_to_all(part, "z", split_axis=0, concat_axis=0, tiled=True))

    partial_out = jnp.dot(
        everyone, w_out, preferred_element_type=F32
    ).astype(BF16)
    shares = lax.axis_size(("grp", "tp"))
    pieces = lax.all_to_all(
        partial_out.reshape(shares, -1, partial_out.shape[1]), ("grp", "tp"), split_axis=0, concat_axis=0, tiled=True
    )
    dec_out = jnp.sum(pieces.astype(F32), axis=0).astype(BF16)
    pre_out = merge(parts, stretch)
    return (pre_out, dec_out.reshape(-1, 2, dec_out.shape[1]))


def solution(mesh):
    shape = mesh.devices.shape
    fine = jax.sharding.Mesh(mesh.devices.reshape(-1, Z_CHIPS, CORES, *shape[1:]), (*CTX, *mesh.axis_names[1:]))
    placed = (
        P(CTX, ("grp", "tp")),
        P(CTX, None, ("grp", "tp")),
        P(CTX, None, ("grp", "tp")),
        P(CTX, None, ("grp", "tp")),
        P(CTX, None, None, ("grp", "tp")),
        P(CTX, None, None, ("grp", "tp")),
        P(),
        P(CTX),
        P(("grp", "tp"), CTX),
    )
    return jax.shard_map(
        shards,
        mesh=fine,
        in_specs=placed,
        out_specs=(P(CTX, ("grp", "tp")), P(("grp", "tp"), None, CTX)),
        check_vma=False,
    )
```

time: 400 us -> 199 us (0.50)
  waiting for transfers between devices: 199 us -> 46.9 us
  matrix products: 58.3 us -> 0.96 us
  Pallas kernels: 0 us -> 41 us
  local copies, waits for them, and re-layouts: 42.5 us -> 7.44 us
  other arithmetic: 27.4 us -> 2.07 us
  blocking collectives: 42 us -> 60.6 us
  starting transfers between devices: 12.9 us -> 24.7 us
    all_gather x2, waiting for transfers between devices: 127 us -> 0.03 us  [the longest x1 0.02 us: shards(): kv_all = lax.all_gather(kv, ('y', 'core'), axis=0)]
    dot_general x25 -> x1, matrix products: 58.3 us -> 0.96 us  [shards(): jnp.dot(everyone, w_out, preferred_element_type=F32).astype(BF16)]
    pallas_call x0 -> x6, Pallas kernels: none -> 41 us  [the longest x2 34.8 us: attend(): pl.pallas_call(functools.partial(attend_body, first_head), out_shape=jax....]
    reduce_scatter x1 -> x0, waiting for transfers between devices: 22.7 us -> none  [shards(): lax.psum_scatter(partial_out.astype(jnp.bfloat16), ('grp', 'tp'), scatter...]
    all_to_all x0 -> x1, blocking collectives: none -> 20.8 us  [shards(): lax.all_to_all(part, 'z', split_axis=0, concat_axis=0, tiled=True)]
    gather x6 -> x0, local copies, waits for them, and re-layouts: 19.7 us -> none  [the longest x4 7.28 us: shards(): jnp.take_along_axis(table_all, arrival_all, axis=1)]
    slice x2 -> x1, local copies, waits for them, and re-layouts: 15.7 us -> 0.75 us  [shards(): asked = jnp.where((row_of == r)[:, None, None], q_rows[r][None], asked)]
    reduce_sum x12 -> x5, other arithmetic: 15.9 us -> 1.02 us  [the longest x1 0.74 us: shards(): jnp.sum(jnp.where(row_of[:, None] == own_rows[None, :], cache_len[None, :...]
  transfers between devices with their start and end apart: 4 -> 6, of which waited for: 3 -> 3; matrix products, arithmetic and copies ran while one was open for 5% -> 3% of each run, Pallas kernels for 0% -> 20%
where the time goes in v1:
time: 199 us; the launch traced here: 198 us
  blocking collectives  60.6 us (30%)
  waiting for transfers between devices  46.9 us (24%)
  Pallas kernels  41 us (21%)
  starting transfers between devices  24.7 us (12%)
  between operations  14.3 us (7%)
  local copies, waits for them, and re-layouts  7.44 us (4%)
  other arithmetic  2.07 us (1%)
    all_gather x1, blocking collectives, shards(): everyone = lax.all_gather(attn, CTX, axis=0, tiled=True)  39.8 us
    pallas_call x2, Pallas kernels, attend(): pl.pallas_call(functools.partial(attend_body, first_head), out_shape=jax....  34.8 us
    all_to_all x1, blocking collectives, shards(): lax.all_to_all(part, 'z', split_axis=0, concat_axis=0, tiled=True)  20.8 us
    all_to_all x1, waiting for transfers between devices, shards(): lax.all_to_all(part, 'z', split_axis=0, concat_axis=0, tiled=True)  17.4 us
    all_to_all x1, waiting for transfers between devices, shards(): ask = lax.all_to_all(ask, CTX, split_axis=0, concat_axis=0, tiled=True)  15.6 us
    all_to_all x1, waiting for transfers between devices, shards(): lax.all_to_all(look_out, CTX, split_axis=0, concat_axis=0, tiled=True)  13.2 us
    all_to_all x1, starting transfers between devices, shards(): ask = lax.all_to_all(ask, CTX, split_axis=0, concat_axis=0, tiled=True)  12.7 us
    unnamed x19, local copies, waits for them, and re-layouts  5.65 us
  transfers between devices with their start and end apart: 6, of which 3 were waited for; matrix products, arithmetic and copies ran while one was open for 3% of the time, Pallas kernels for 20%

profile of v1, /device:TPU:1, one launch (start us, length us, event | category | flops | bytes accessed | tf_op | source)
XLA Modules:
  0.0 197.9 jit_solution(9031641515345442506)
XLA Ops:
  7.2 0.7 all-gather.5.cloned.1.call-update
  8.0 1.1 copy-done.2
  9.1 0.8 copy-done.3
  9.8 1.3 split_keys_values.1
  11.2 0.8 fusion.13
  12.0 0.8 copy.13
  12.9 0.1 select_reduce_fusion
  13.1 0.7 select_reduce_fusion.1
  13.8 0.2 select_select_fusion
  14.0 0.1 broadcast_in_dim.113
  14.1 0.7 pad_maximum_fusion
  14.8 12.7 %all-to-all-start = ((bf16[32,32,128]{2,1,0:T(8,128)(2,1)}), bf16[32,32,128]{2,1,0:T(8,128)(2,1)S(1)}, u32[]{:S(2)}, u32[]{:S(2)}) async-start(bf16[32,32,128]{2,1,0:T(8,128)(2,1)} %pad_maximum_fusion), calls=%async_computation | async-start | bytes 524288 | tf_op jit(solution)/shard_map/all_to_all | solution.py:395
  27.6 0.1 reduce_sum.48
  27.7 0.1 reduce_sum.49.place_ref
  27.8 15.6 %all-to-all-done.ask_ref = bf16[32,32,128]{2,1,0:T(8,128)(2,1)S(1)} async-done(((bf16[32,32,128]{2,1,0:T(8,128)(2,1)}), bf16[32,32,128]{2,1,0:T(8,128)(2,1)S(1)}, u32[]{:S(2)}, u32[]{:S(2)}) %all-to-all-start) | async-done | bytes 262176 | tf_op jit(solution)/shard_map/all_to_all | solution.py:395
  43.5 2.6 %look_in_blocks.1 = bf16[32,32,128]{2,1,0:T(8,128)(2,1)} custom-call(s32[32]{0:T(128)S(1)} %reduce_sum.49.place_ref, bf16[32,32,128]{2,1,0:T(8,128)(2,1)S(1)} %all-to-all-done.ask_ref, bf16[32,256,128]{2,1,0:T(8,128)(2,1)S(1)} %bitcast.11), custom_call_target="tpu_custom_call" | custom-call | flops 536870912 | bytes 2097152 | tf_op jit(solution)/shard_map/look_in_blocks/pallas_call | solution.py:266
  46.0 4.0 %all-to-all-start.1 = ((bf16[32,32,128]{2,1,0:T(8,128)(2,1)}), bf16[32,32,128]{2,1,0:T(8,128)(2,1)S(1)}, u32[]{:S(2)}, u32[]{:S(2)}) async-start(bf16[32,32,128]{2,1,0:T(8,128)(2,1)} %look_in_blocks.1), calls=%async_computation.1 | async-start | bytes 524288 | tf_op jit(solution)/shard_map/all_to_all | solution.py:398
  50.2 0.1 mul.54.deltas_ref
  50.3 13.2 %all-to-all-done.1.answer_ref = bf16[32,32,128]{2,1,0:T(8,128)(2,1)S(1)} async-done(((bf16[32,32,128]{2,1,0:T(8,128)(2,1)}), bf16[32,32,128]{2,1,0:T(8,128)(2,1)S(1)}, u32[]{:S(2)}, u32[]{:S(2)}) %all-to-all-start.1) | async-done | bytes 262176 | tf_op jit(solution)/shard_map/all_to_all | solution.py:398
  63.5 1.0 gather_answers.1
  64.5 39.8 %all_gather.19 = bf16[256,1024]{1,0:T(8,128)(2,1)S(1)} all-gather(bf16[8,1024]{1,0:T(8,128)(2,1)S(1)} %gather_answers.1), channel_id=1, replica_groups=mesh['y'=2,'z'=8,'core'=2,'grp'=2,'tp'=4] {'y','z','core'}, dimensions={0}, use_global_device_ids=true | all-gather | bytes 540672 | tf_op jit(solution)/shard_map/all_gather | solution.py:400
  104.3 1.0 convolution_convert_fusion
  105.2 4.3 %all-to-all-start.4 = ((bf16[8,32,256]{2,1,0:T(8,128)(2,1)}), bf16[8,32,256]{2,1,0:T(8,128)(2,1)S(1)}, u32[]{:S(2)}, u32[]{:S(2)}) async-start(bf16[8,32,256]{2,1,0:T(8,128)(2,1)} %bitcast.7), calls=%async_computation.4 | async-start | bytes 262144 | tf_op jit(solution)/shard_map/all_to_all | solution.py:419
  109.6 1.8 copy-done.5
  111.4 1.2 copy-done.6
  112.6 17.7 %attend.2 = bf16[8,288,128]{2,1,0:T(8,128)(2,1)} custom-call(s32[32]{0:T(128)S(1)} %mul.54.deltas_ref, bf16[8,64,1024]{2,1,0:T(8,128)(2,1)S(1)} %bitcast.17, bf16[4,2,1344,128]{3,2,1,0:T(8,128)(2,1)S(1)} %bitcast.15), custom_call_target="tpu_custom_call" | custom-call | flops 11274289152 | bytes 2752512 | tf_op jit(solution)/shard_map/attend/pallas_call | solution.py:167
  130.3 17.1 %attend.3 = bf16[8,288,128]{2,1,0:T(8,128)(2,1)S(1)} custom-call(s32[32]{0:T(128)S(1)} %mul.54.deltas_ref, bf16[8,64,1024]{2,1,0:T(8,128)(2,1)S(1)} %bitcast.18, bf16[4,2,1344,128]{3,2,1,0:T(8,128)(2,1)S(1)} %bitcast.16), custom_call_target="tpu_custom_call" | custom-call | flops 11274289152 | bytes 2752512 | tf_op jit(solution)/shard_map/attend/pallas_call | solution.py:167
  147.4 20.8 %all_to_all.25.refs_1_ = bf16[8,288,128]{2,1,0:T(8,128)(2,1)S(1)} all-to-all(bf16[8,288,128]{2,1,0:T(8,128)(2,1)S(1)} %attend.3), channel_id=1, replica_groups=mesh['y'=2,'z'=8,'core'=2,'grp'=2,'tp'=4] {'z'}, dimensions={0} | all-to-all | bytes 1179648 | tf_op jit(solution)/shard_map/all_to_all | solution.py:413
  168.2 3.5 %all-to-all-start.2 = ((bf16[8,288,128]{2,1,0:T(8,128)(2,1)}), bf16[8,288,128]{2,1,0:T(8,128)(2,1)S(1)}, u32[]{:S(2)}, u32[]{:S(2)}) async-start(bf16[8,288,128]{2,1,0:T(8,128)(2,1)} %attend.2), calls=%async_computation.2 | async-start | bytes 1179648 | tf_op jit(solution)/shard_map/all_to_all | solution.py:413
  171.7 0.6 reshape.141
  172.4 17.4 %all-to-all-done.2.refs_0_ = bf16[8,288,128]{2,1,0:T(8,128)(2,1)S(1)} async-done(((bf16[8,288,128]{2,1,0:T(8,128)(2,1)}), bf16[8,288,128]{2,1,0:T(8,128)(2,1)S(1)}, u32[]{:S(2)}, u32[]{:S(2)}) %all-to-all-start.2) | async-done | bytes 589856 | tf_op jit(solution)/shard_map/all_to_all | solution.py:413
  189.8 1.3 merge_parts.1
  (37 shorter events, 0.5 us)
Async XLA Ops:
  7.2 97.1 %copy-start = (bf16[1024,256]{1,0:T(8,128)(2,1)S(1)}, bf16[1024,256]{1,0:T(8,128)(2,1)}, u32[]{:S(2)}) copy-start(bf16[1024,256]{1,0:T(8,128)(2,1)} %param.17) | copy-start | bytes 1572868
  7.2 36.3 %copy-start.1 = (bf16[32,128,2,128]{3,2,1,0:T(2,128)(2,1)S(1)}, bf16[32,128,2,128]{3,2,1,0:T(2,128)(2,1)}, u32[]{:S(2)}) copy-start(bf16[32,128,2,128]{3,2,1,0:T(2,128)(2,1)} %param.14) | copy-start | bytes 6291460
  7.2 102.4 %all-gather.5.cloned.1.call-start = ((), (), s32[]{:S(2)}) async-start(), calls=%async_computation.5 | async-start | bytes 1179648 | tf_op jit(solution)/shard_map/all_gather | solution.py:365
  7.9 101.6 %all-gather.7.cloned.1.call-start = ((), (), s32[]{:S(2)}) async-start(), calls=%async_computation.6 | async-start | bytes 3440640 | tf_op jit(solution)/shard_map/all_gather | solution.py:369
  8.0 1.1 copy-start.2
  9.1 0.8 copy-start.3
  9.8 17.8 %copy-start.8 = (s32[128,8]{0,1:T(8,128)S(1)}, s32[128,8]{0,1:T(8,128)}, u32[]{:S(2)}) copy-start(s32[128,8]{0,1:T(8,128)} %param.15) | copy-start | bytes 12292
  11.2 38.9 %copy-start.7 = (bf16[4,2,1024]{2,1,0:T(2,128)(2,1)S(1)}, bf16[4,2,1024]{2,1,0:T(2,128)(2,1)}, u32[]{:S(2)}) copy-start(bf16[4,2,1024]{2,1,0:T(2,128)(2,1)} %param.12) | copy-start | bytes 49156
  11.2 52.3 %copy-start.4 = (bf16[4,2,2,128]{3,2,1,0:T(2,128)(2,1)S(1)}, bf16[4,2,2,128]{3,2,1,0:T(2,128)(2,1)}, u32[]{:S(2)}) copy-start(bf16[4,2,2,128]{3,2,1,0:T(2,128)(2,1)} %param.13) | copy-start | bytes 12292
  14.8 28.6 %all-to-all-start = ((bf16[32,32,128]{2,1,0:T(8,128)(2,1)}), bf16[32,32,128]{2,1,0:T(8,128)(2,1)S(1)}, u32[]{:S(2)}, u32[]{:S(2)}) async-start(bf16[32,32,128]{2,1,0:T(8,128)(2,1)} %pad_maximum_fusion), calls=%async_computation | async-start | bytes 524288 | tf_op jit(solution)/shard_map/all_to_all | solution.py:395
  46.0 17.4 %all-to-all-start.1 = ((bf16[32,32,128]{2,1,0:T(8,128)(2,1)}), bf16[32,32,128]{2,1,0:T(8,128)(2,1)S(1)}, u32[]{:S(2)}, u32[]{:S(2)}) async-start(bf16[32,32,128]{2,1,0:T(8,128)(2,1)} %look_in_blocks.1), calls=%async_computation.1 | async-start | bytes 524288 | tf_op jit(solution)/shard_map/all_to_all | solution.py:398
  105.2 42.1 %all-to-all-start.4 = ((bf16[8,32,256]{2,1,0:T(8,128)(2,1)}), bf16[8,32,256]{2,1,0:T(8,128)(2,1)S(1)}, u32[]{:S(2)}, u32[]{:S(2)}) async-start(bf16[8,32,256]{2,1,0:T(8,128)(2,1)} %bitcast.7), calls=%async_computation.4 | async-start | bytes 262144 | tf_op jit(solution)/shard_map/all_to_all | solution.py:419
  109.6 1.8 copy-start.5
  111.4 1.2 copy-start.6
  168.2 21.6 %all-to-all-start.2 = ((bf16[8,288,128]{2,1,0:T(8,128)(2,1)}), bf16[8,288,128]{2,1,0:T(8,128)(2,1)S(1)}, u32[]{:S(2)}, u32[]{:S(2)}) async-start(bf16[8,288,128]{2,1,0:T(8,128)(2,1)} %attend.2), calls=%async_computation.2 | async-start | bytes 1179648 | tf_op jit(solution)/shard_map/all_to_all | solution.py:413
Sparse Core Ops, SparseCore 0:
  9.8 41.5 all-gather.4
  53.2 37.1 all-gather.6
